TPU v7x, 32 devices: a whole 2x2x4 slice. The times are simulated.
32 devices in a mesh: group: 4 (over y, core), dev: 8 (over z, x).
Axes of the slice: x: 2, y: 2, z: 4, core: 2. Of those that a mesh axis runs over, the one named last changes fastest.
Arguments:
- primary_q: bfloat16 [64, 3584, 1024], P(('group', 'dev')), may hold values from -0.09375 to 0.09375
- primary_scales: bfloat16 [64, 28, 8], P(('group', 'dev')), may hold values from 0.5 to 2
- new_place: int32 [32], P(('group', 'dev')), may hold values from 0 to 63, as said below
- tokens: bfloat16 [512, 3584], P(('group', 'dev')), may hold values from -6 to 6
- experts: int32 [512, 8], P(('group', 'dev')), may hold values from 0 to 63, all different within a row
- replica: int32 [512, 8], P(('group', 'dev')), may hold values from 0 to 1
- route_num: int32 [512, 8], P(('group', 'dev')), may hold values from 1 to 16
Outputs:
- new_weights: bfloat16 [32, 3584, 1024], P(('group', 'dev'))
- new_scales: bfloat16 [32, 28, 8], P(('group', 'dev'))
- hidden_out: bfloat16 [512, 8, 1024], P(('group', 'dev'))
- slot_load: int32 [32, 3], P(('group', 'dev'))
Inputs may be any that keep to these rules, and one draw needn't show every extreme that they name: `new_place`: the redundant slots of the 8 devices of one group hold 8 different experts, each with its primary copy on a device of that group.
All inputs are finite; a program needn't handle non-finite values.
Results may differ from a plain program's by a relative error of at most 0.0057.
Values may be sent and summed in bfloat16 or wider, within the bound.
No kernel may reach another device: no remote copies, remote signals or barrier semaphores. Data moves between devices by JAX's collectives and lax.ppermute only.
A program may use at most 192 MiB of HBM per device.

v0:
```python
import functools

import jax
import jax.numpy as jnp
from jax import lax
from jax.experimental import pallas as pl
from jax.experimental.pallas import tpu as pltpu
from jax.sharding import PartitionSpec as P

TILE = 128
CAP = 2
POOL = 16
ROW_CHIPS = 4
COMMON = 8
VMEM_LIMIT = 60 * 1024 * 1024
AXES = ("group", "dev")
PARTS = (112, 112)


def expert_kernel(x_ref, q_ref, s_ref, o_ref, acc_ref):
    step = pl.program_id(0)

    @pl.when(step == 0)
    def _():
        acc_ref[...] = jnp.zeros_like(acc_ref)

    holding, depth, _ = q_ref.shape
    cells = 2 * CAP
    rows = x_ref.shape[0]
    member_of = lax.broadcasted_iota(jnp.int32, (rows, TILE), 0) // cells % holding
    total = acc_ref[...]
    for member in range(holding):
        for block in range(depth // TILE):
            span = slice(block * TILE, (block + 1) * TILE)
            scale = s_ref[member, 0, block : block + 1, :]
            weights = (q_ref[member, span, :].astype(jnp.float32) * scale).astype(jnp.bfloat16)
            rows_in = jnp.where(member_of == member, x_ref[:, span], jnp.zeros((), jnp.bfloat16))
            total = total + jnp.dot(rows_in, weights, preferred_element_type=jnp.float32)
    acc_ref[...] = total

    @pl.when(step == pl.num_programs(0) - 1)
    def _():
        value = acc_ref[...]
        o_ref[...] = (value / (1.0 + jnp.exp(-value))).astype(jnp.bfloat16)


def serve(rows, values, scales):
    holding, width_in, hidden = values.shape
    depth = 512
    steps = width_in // depth
    count = rows.shape[0]
    wide = jnp.repeat(scales.astype(jnp.float32), TILE, axis=2)
    wide = wide.reshape(holding, steps, depth // TILE, hidden)
    return pl.pallas_call(
        expert_kernel,
        grid=(steps,),
        in_specs=[
            pl.BlockSpec((count, depth), lambda k: (0, k)),
            pl.BlockSpec((holding, depth, hidden), lambda k: (0, k, 0)),
            pl.BlockSpec((holding, 1, depth // TILE, hidden), lambda k: (0, k, 0, 0)),
        ],
        out_specs=pl.BlockSpec((count, hidden), lambda k: (0, 0)),
        out_shape=jax.ShapeDtypeStruct((count, hidden), jnp.bfloat16),
        scratch_shapes=[pltpu.VMEM((count, hidden), jnp.float32)],
        compiler_params=pltpu.CompilerParams(vmem_limit_bytes=VMEM_LIMIT),
        cost_estimate=pl.CostEstimate(
            flops=2 * count * width_in * hidden * holding,
            bytes_accessed=2 * (values.size + count * (width_in + hidden)),
            transcendentals=count * hidden,
        ),
    )(rows, values, wide)


def through_vmem(count, sources, out_at, held, in_sem, out_sem):
    def leave(spot):
        pltpu.make_async_copy(held.at[spot], held.at[spot], in_sem.at[spot]).wait()
        pltpu.make_async_copy(held.at[spot], out_at(spot), out_sem.at[spot]).start()

    def finish(spot):
        pltpu.make_async_copy(held.at[spot], out_at(spot), out_sem.at[spot]).wait()

    for stage in (sources, leave, finish):
        pl.loop(0, count)(stage)


def gather_kernel(index_ref, *refs):
    *source_refs, out_ref, held, in_sem, out_sem = refs

    def start(spot):
        index = index_ref[spot]
        base = 0
        for source_ref in source_refs:
            count = source_ref.shape[0]
            inside = (index >= base) & (index < base + count)
            at = jnp.clip(index - base, 0, count - 1)

            @pl.when(inside)
            def _():
                pltpu.make_async_copy(
                    source_ref.at[at], held.at[spot], in_sem.at[spot]
                ).start()

            base += count

    through_vmem(out_ref.shape[0], start, lambda spot: out_ref.at[spot], held, in_sem, out_sem)


def gather(indices, *sources):
    count = indices.shape[0]
    indices = jnp.clip(indices, 0, sum(source.shape[0] for source in sources) - 1)
    anywhere = pl.BlockSpec(memory_space=pl.ANY)
    out = jax.ShapeDtypeStruct((count,) + sources[0].shape[1:], sources[0].dtype)
    return pl.pallas_call(
        gather_kernel,
        in_specs=[pl.BlockSpec(memory_space=pltpu.SMEM)] + [anywhere] * len(sources),
        out_specs=anywhere,
        out_shape=out,
        scratch_shapes=[
            pltpu.VMEM(out.shape, out.dtype),
            pltpu.SemaphoreType.DMA((count,)),
            pltpu.SemaphoreType.DMA((count,)),
        ],
        compiler_params=pltpu.CompilerParams(vmem_limit_bytes=VMEM_LIMIT),
        cost_estimate=pl.CostEstimate(flops=0, bytes_accessed=4 * out.size, transcendentals=0),
    )(indices, *sources)


def chunk_kernel(first, in_ref, out_ref, held, in_sem, out_sem):
    height = out_ref.shape[2]

    def start(spot):
        pltpu.make_async_copy(
            in_ref.at[:, pl.ds(first + spot * height, height), :], held.at[spot], in_sem.at[spot]
        ).start()

    through_vmem(POOL, start, lambda spot: out_ref.at[spot], held, in_sem, out_sem)


def by_chunk(values, first, height):
    holding, _, hidden = values.shape
    anywhere = pl.BlockSpec(memory_space=pl.ANY)
    out = jax.ShapeDtypeStruct((POOL, holding, height, hidden), values.dtype)
    return pl.pallas_call(
        functools.partial(chunk_kernel, first),
        in_specs=[anywhere],
        out_specs=anywhere,
        out_shape=out,
        scratch_shapes=[
            pltpu.VMEM(out.shape, out.dtype),
            pltpu.SemaphoreType.DMA((POOL,)),
            pltpu.SemaphoreType.DMA((POOL,)),
        ],
        compiler_params=pltpu.CompilerParams(vmem_limit_bytes=VMEM_LIMIT),
        cost_estimate=pl.CostEstimate(
            flops=0, bytes_accessed=4 * out.size, transcendentals=0
        ),
    )(values)


def join_kernel(first, blocks_ref, *refs):
    out_ref, held, in_sem, out_sem = refs[-4:]
    count, height, _ = blocks_ref.shape

    def start(spot):
        pltpu.make_async_copy(blocks_ref.at[spot], held.at[spot], in_sem.at[spot]).start()

    def out_at(spot):
        return out_ref.at[0, pl.ds(first + spot * height, height), :]

    through_vmem(count, start, out_at, held, in_sem, out_sem)


def join(weights, blocks, first, width_in):
    count, _, hidden = blocks.shape
    anywhere = pl.BlockSpec(memory_space=pl.ANY)
    operands = (blocks,) if weights is None else (blocks, weights)
    return pl.pallas_call(
        functools.partial(join_kernel, first),
        in_specs=[anywhere] * len(operands),
        out_specs=anywhere,
        out_shape=jax.ShapeDtypeStruct((1, width_in, hidden), blocks.dtype),
        input_output_aliases={} if weights is None else {1: 0},
        scratch_shapes=[
            pltpu.VMEM(blocks.shape, blocks.dtype),
            pltpu.SemaphoreType.DMA((count,)),
            pltpu.SemaphoreType.DMA((count,)),
        ],
        compiler_params=pltpu.CompilerParams(vmem_limit_bytes=VMEM_LIMIT),
        cost_estimate=pl.CostEstimate(flops=0, bytes_accessed=4 * blocks.size, transcendentals=0),
    )(*operands)


def late_over(count, leave_rows, block, pairs):
    most = POOL - COMMON

    def branch_of(size):
        def branch(leave_rows, block):
            if size == 0:
                return jnp.zeros((most,) + block.shape[1:], block.dtype)
            late = gather(leave_rows[COMMON : COMMON + size], block)
            got = lax.ppermute(late, AXES, pairs)
            return jnp.pad(got, ((0, most - size), (0, 0), (0, 0)))

        return branch

    branches = [branch_of(size) for size in range(most + 1)]
    return lax.switch(jnp.maximum(count - COMMON, 0), branches, leave_rows, block)


def route(experts, replica, place_all, holding):
    pair_count = experts.shape[1]
    device_ids = jnp.arange(place_all.shape[0], dtype=jnp.int32)
    matched = experts[:, :, None] == place_all[None, None, :]
    has_copy = jnp.any(matched, axis=2)
    holder = jnp.sum(jnp.where(matched, device_ids[None, None, :], 0), axis=2)
    use_copy = (replica == 1) & has_copy
    target = jnp.where(use_copy, holder, experts // holding)
    slot_id = jnp.where(use_copy, holding, experts % holding)
    pair_order = jnp.arange(pair_count)
    before = pair_order[:, None] < pair_order[None, :]
    position = jnp.sum((target[:, :, None] == target[:, None, :]) & before[None], axis=1)
    cell = experts % holding * (2 * CAP) + use_copy * CAP + position
    return target, slot_id, position < CAP, cell


def per_device(primary_q, primary_scales, new_place, tokens, experts, replica, route_num):
    holding, width_in, hidden = primary_q.shape
    dev_count = lax.axis_size("dev")
    group_count = lax.axis_size("group")
    device_count = dev_count * group_count
    half = dev_count // 2
    pooled = POOL // half
    my_dev = lax.axis_index("dev")
    my_group = lax.axis_index("group")
    first_dev = my_group * dev_count
    pools = [
        [(base + group) * dev_count + side * half + spot for group in range(pooled) for spot in range(half)]
        for base in range(0, group_count, pooled)
        for side in range(2)
    ]
    over = [
        (group * dev_count + spot, group * dev_count + (spot + half) % dev_count)
        for group in range(group_count)
        for spot in range(dev_count)
    ]

    device_ids = jnp.arange(device_count, dtype=jnp.int32)
    my_id = first_dev + my_dev

    row_count, top_count = experts.shape
    pair_count = row_count * top_count
    scale_cols = primary_scales.size // row_count
    notice = jnp.concatenate(
        [
            experts.astype(jnp.bfloat16),
            replica.astype(jnp.bfloat16),
            primary_scales.reshape(row_count, scale_cols),
        ],
        axis=1,
    )
    notice = jnp.pad(notice, ((0, 0), (0, -notice.shape[1] % TILE)))
    held = jnp.concatenate([tokens, notice], axis=1)
    dev_bits = dev_count.bit_length() - 1
    all_bits = device_count.bit_length() - 1
    order = list(range(dev_bits))[::-1] + list(range(dev_bits, all_bits))[::-1]
    apart = device_ids ^ my_id
    spot_of = sum((apart >> bit & 1) << step for step, bit in enumerate(order))

    def double(held, bits):
        for bit in bits:
            pairs = [(device, device ^ 1 << bit) for device in range(device_count)]
            held = jnp.concatenate([held, lax.ppermute(held, AXES, pairs)], axis=0)
        return held

    first_height, second_height = PARTS
    held = double(held, order[:1])
    first, held = lax.optimization_barrier((by_chunk(primary_q, 0, first_height), held))
    held = double(held, order[1:2])
    place_all = jnp.broadcast_to(new_place.astype(jnp.bfloat16), (device_count, TILE))
    place_all, held = lax.optimization_barrier((place_all, held))
    held = double(held, order[2:dev_bits])

    place_all = lax.all_to_all(
        place_all,
        AXES,
        split_axis=0,
        concat_axis=0,
        tiled=True,
    )

    place_all = place_all[:, 0].astype(jnp.int32)
    source = place_all // holding
    dest_side = device_ids % dev_count // half
    source_side = source % dev_count // half
    crossing = source_side != dest_side
    source_row = (source // dev_count % pooled * half + source % half) * holding + place_all % holding
    pool_of = device_ids // dev_count // pooled
    peers = (pool_of[:, None] == pool_of[None, :]) & (dest_side[:, None] == dest_side[None, :])
    ahead = peers & crossing[None, :] & (device_ids[None, :] < device_ids[:, None])
    rank = jnp.sum(ahead, axis=1)
    cross_count = jnp.max(jnp.where(crossing, rank + 1, 0))
    my_side = my_dev // half
    my_pool = my_group // pooled
    leaving = (pool_of == my_pool) & (dest_side != my_side) & crossing
    slots = jnp.arange(POOL)
    leave_rows = jnp.sum(
        jnp.where(leaving[None, :] & (rank[None, :] == slots[:, None]), source_row[None, :], 0), axis=1
    )
    staying = (pool_of == my_pool) & (dest_side == my_side)
    place_in_pool = device_ids // dev_count % pooled * half + device_ids % half
    give_rows = jnp.sum(
        jnp.where(
            staying[None, :] & (place_in_pool[None, :] == slots[:, None]),
            jnp.where(crossing, POOL * holding + rank, source_row)[None, :],
            0,
        ),
        axis=1,
    )

    def spread_over(block):
        block = lax.all_to_all(
            block, AXES, split_axis=0, concat_axis=0, tiled=True, axis_index_groups=pools
        )
        return block.reshape((POOL * holding,) + block.shape[2:])

    first, held, place_all, leave_rows, give_rows, cross_count = lax.optimization_barrier(
        (first, held, place_all, leave_rows, give_rows, cross_count)
    )
    first = spread_over(first)
    second = by_chunk(primary_q, POOL * first_height, second_height)
    held, second = lax.optimization_barrier((held, second))
    held = double(held, order[dev_bits:-1])
    held, second = lax.optimization_barrier((held, second))
    second = spread_over(second)

    cells = 2 * CAP
    cell_count = device_count * holding * cells

    def pairs_of(held):
        notices = held[:, width_in:].reshape(device_count, row_count, -1)[spot_of]
        experts_all = notices[:, :, :top_count].astype(jnp.int32)
        replica_all = notices[:, :, top_count : 2 * top_count].astype(jnp.int32)
        return [each.reshape(device_count, pair_count) for each in (experts_all, replica_all)]

    def work(held, place_all, values, scales):
        experts_all, replica_all = pairs_of(held)
        _, _, served, cell = route(experts_all, replica_all, place_all, holding)
        mine = served & (experts_all // holding == my_id)
        cell_ids = jnp.arange(holding * cells)
        hit = mine[:, None, :] & (cell[:, None, :] == cell_ids[None, :, None])
        row_at = spot_of[:, None] * row_count + jnp.sum(
            jnp.where(hit, jnp.arange(pair_count) // top_count, 0), axis=2
        )
        row_at = jnp.where(jnp.any(hit, axis=2), row_at, -1).reshape(cell_count)
        row_hits = row_at[:, None] == jnp.arange(device_count * row_count)[None, :]
        rows = jnp.dot(row_hits.astype(jnp.bfloat16), held, preferred_element_type=jnp.float32)
        return serve(rows.astype(jnp.bfloat16), values, scales)

    sent = gather(leave_rows[:COMMON], first)
    sent, held = lax.optimization_barrier((sent, held))
    common = lax.ppermute(sent, AXES, over)
    held = double(held, order[-1:])
    activated = work(held, place_all, primary_q, primary_scales)

    columns = dev_count // ROW_CHIPS

    def exchange(blocks, axis, mine, stride, within):
        got = [lax.dynamic_index_in_dim(blocks, mine, axis, keepdims=False)]
        for step in range(1, blocks.shape[axis]):
            pairs = [
                (device, device ^ step * stride) for device in range(device_count)
            ]
            block = lax.dynamic_index_in_dim(blocks, mine ^ step, axis, keepdims=False)
            got.append(lax.ppermute(block, AXES, pairs))
        return jnp.stack(got, axis=within)

    blocks = activated.reshape(group_count, ROW_CHIPS, columns, holding * cells, hidden)
    blocks = exchange(blocks, 1, my_dev // columns, columns, 1)
    leave_rows, blocks = lax.optimization_barrier((leave_rows, blocks))
    late = late_over(cross_count, leave_rows, first, over)
    first = gather(give_rows, first, common, late)
    first, leave_rows, blocks = lax.optimization_barrier((first, leave_rows, blocks))
    sent = gather(leave_rows[:COMMON], second)
    sent, blocks = lax.optimization_barrier((sent, blocks))
    common = lax.ppermute(sent, AXES, over)
    blocks = exchange(blocks, 2, my_dev % columns, 1, 1)
    returned = exchange(blocks, 0, my_group, dev_count, 0)
    leave_rows, returned = lax.optimization_barrier((leave_rows, returned))
    first = lax.all_to_all(
        first, AXES, split_axis=0, concat_axis=0, tiled=True, axis_index_groups=pools
    )
    late = late_over(cross_count, leave_rows, second, over)
    second = gather(give_rows, second, common, late)
    second, held = lax.optimization_barrier((second, held))
    second = lax.all_to_all(
        second, AXES, split_axis=0, concat_axis=0, tiled=True, axis_index_groups=pools
    )
    new_weights = join(None, first, 0, width_in)
    new_weights = join(new_weights, second, first.shape[0] * first.shape[1], width_in)

    experts_all, replica_all = pairs_of(held)
    target, slot_id, served, _ = route(experts_all, replica_all, place_all, holding)
    arriving = served & (target == my_id)
    slot_load = jnp.stack(
        [jnp.sum((arriving & (slot_id == slot)).astype(jnp.int32)) for slot in range(holding + 1)]
    )[None]
    owner_notice = held[:, width_in:].reshape(device_count, row_count, -1)
    owner_notice = lax.dynamic_index_in_dim(
        owner_notice, spot_of[new_place[0] // holding], 0, keepdims=False
    )
    owner_scales = owner_notice[:, 2 * top_count : 2 * top_count + scale_cols]
    new_scales = lax.dynamic_index_in_dim(
        owner_scales.reshape(primary_scales.shape), new_place[0] % holding, 0
    )

    my_experts = experts.reshape(1, pair_count)
    _, _, my_served, my_cell = route(
        my_experts, replica.reshape(1, pair_count), place_all, holding
    )
    their_id = my_experts // holding
    apart = their_id ^ my_id
    block_at = apart // dev_count * columns + apart % columns
    block_at = block_at * ROW_CHIPS + apart % dev_count // columns
    my_cell = (block_at * (holding * cells) + my_cell)[0]
    placed = (my_cell[:, None] == jnp.arange(cell_count)[None, :]) & my_served[0][:, None]
    selected = jnp.dot(
        placed.astype(jnp.bfloat16),
        returned.reshape(cell_count, hidden),
        preferred_element_type=jnp.float32,
    )
    weight = route_num.reshape(pair_count).astype(jnp.float32) / 16.0
    hidden_out = (selected * weight[:, None]).astype(jnp.bfloat16)
    hidden_out = hidden_out.reshape(row_count, top_count, hidden)
    return (new_weights, new_scales, hidden_out, slot_load)


def solution(mesh):
    in_specs = (
        P(AXES, None, None),
        P(AXES, None, None),
        P(AXES),
        P(AXES, None),
        P(AXES, None),
        P(AXES, None),
        P(AXES, None),
    )
    out_specs = (
        P(AXES, None, None),
        P(AXES, None, None),
        P(AXES, None, None),
        P(AXES, None),
    )
    return jax.shard_map(
        per_device, mesh=mesh, in_specs=in_specs, out_specs=out_specs, check_vma=False
    )
```

profile of v0, /device:TPU:0, one launch (start us, length us, event | category | flops | bytes accessed | tf_op | source)
XLA Modules:
  0.0 447.9 jit_solution(1883934768196463946)
XLA Ops:
  3.1 0.9 pad_maximum_fusion.6
  4.1 4.1 collective-permute-start.16
  8.2 6.0 %shard_map.102 = bf16[16,2,112,1024]{3,2,1,0:T(8,128)(2,1)} custom-call(bf16[2,3584,1024]{2,1,0:T(8,128)(2,1)} %q_ref.1), custom_call_target="tpu_custom_call" | custom-call | bytes 14680064 | tf_op jit(solution)/shard_map/pallas_call | solution.py:143
  14.2 1.6 collective-permute-start.17
  16.6 5.0 %collective-permute-done.17 = bf16[32,3712]{1,0:T(8,128)(2,1)S(1)} collective-permute-done((bf16[32,3712]{1,0:T(8,128)(2,1)S(1)}, bf16[32,3712]{1,0:T(8,128)(2,1)S(1)}, u32[]{:S(2)}, u32[]{:S(2)}) %collective-permute-start.17) | collective-permute-done | bytes 237600 | tf_op jit(solution)/shard_map/ppermute | solution.py:272
  22.2 6.0 %all-to-all-start = ((bf16[32,1,128]{2,1,0:T(2,128)(2,1)}), bf16[32,1,128]{2,1,0:T(2,128)(2,1)S(1)}, u32[]{:S(2)}, u32[]{:S(2)}) async-start(bf16[32,1,128]{2,1,0:T(2,128)(2,1)} %copy.142), calls=%async_computation | async-start | bytes 32768 | tf_op jit(solution)/shard_map/all_to_all | solution.py:283
  28.2 1.8 collective-permute-start.18
  30.1 5.2 %all-to-all-done = bf16[32,1,128]{2,1,0:T(2,128)(2,1)S(1)} async-done(((bf16[32,1,128]{2,1,0:T(2,128)(2,1)}), bf16[32,1,128]{2,1,0:T(2,128)(2,1)S(1)}, u32[]{:S(2)}, u32[]{:S(2)}) %all-to-all-start) | async-done | bytes 8224 | tf_op jit(solution)/shard_map/all_to_all | solution.py:283
  36.5 5.0 %collective-permute-done.18 = bf16[64,3712]{1,0:T(8,128)(2,1)S(1)} collective-permute-done((bf16[64,3712]{1,0:T(8,128)(2,1)S(1)}, bf16[64,3712]{1,0:T(8,128)(2,1)S(1)}, u32[]{:S(2)}, u32[]{:S(2)}) %collective-permute-start.18) | collective-permute-done | bytes 475168 | tf_op jit(solution)/shard_map/ppermute | solution.py:272
  41.5 4.8 %all-to-all-start.2 = ((bf16[16,2,112,1024]{3,2,1,0:T(8,128)(2,1)}), bf16[16,2,112,1024]{3,2,1,0:T(8,128)(2,1)}, u32[]{:S(2)}, u32[]{:S(2)}) async-start(bf16[16,2,112,1024]{3,2,1,0:T(8,128)(2,1)} %shard_map.102), calls=%async_computation.2 | async-start | bytes 14680064 | tf_op jit(solution)/shard_map/all_to_all | solution.py:321
  46.4 6.0 %shard_map.103 = bf16[16,2,112,1024]{3,2,1,0:T(8,128)(2,1)} custom-call(bf16[2,3584,1024]{2,1,0:T(8,128)(2,1)} %q_ref.1), custom_call_target="tpu_custom_call" | custom-call | bytes 14680064 | tf_op jit(solution)/shard_map/pallas_call | solution.py:143
  52.3 1.9 collective-permute-start.19
  54.3 94.2 %collective-permute-done.19 = bf16[128,3712]{1,0:T(8,128)(2,1)S(1)} collective-permute-done((bf16[128,3712]{1,0:T(8,128)(2,1)S(1)}, bf16[128,3712]{1,0:T(8,128)(2,1)S(1)}, u32[]{:S(2)}, u32[]{:S(2)}) %collective-permute-start.19) | collective-permute-done | bytes 950304 | tf_op jit(solution)/shard_map/ppermute | solution.py:272
  148.6 4.7 %all-to-all-start.1 = ((bf16[16,2,112,1024]{3,2,1,0:T(8,128)(2,1)}), bf16[16,2,112,1024]{3,2,1,0:T(8,128)(2,1)}, u32[]{:S(2)}, u32[]{:S(2)}) async-start(bf16[16,2,112,1024]{3,2,1,0:T(8,128)(2,1)} %shard_map.103), calls=%async_computation.1 | async-start | bytes 14680064 | tf_op jit(solution)/shard_map/all_to_all | solution.py:321
  153.8 3.2 shard_map.104
  159.7 2.5 collective-permute-start.20
  162.3 1.8 constant_dynamic-update-slice_fusion
  164.1 1.8 copy-done
  169.8 4.6 %convolution_convert_fusion.x_ref = bf16[256,3712]{1,0:T(8,128)(2,1)} fusion(bf16[512,3712]{1,0:T(8,128)(2,1)} %copy-done, s32[256]{0:T(256)S(1)} %select_n.540), kind=kOutput, calls=%fused_computation.16 | convolution fusion | flops 974159872 | bytes 5702656 | tf_op jit(solution)/shard_map/dot_general | solution.py:356
  174.3 13.0 %shard_map.105 = bf16[256,1024]{1,0:T(8,128)(2,1)} custom-call(bf16[256,3712]{1,0:T(8,128)(2,1)} %convolution_convert_fusion.x_ref, bf16[2,3584,1024]{2,1,0:T(8,128)(2,1)} %q_ref.1, f32[2,7,4,1024]{3,2,1,0:T(4,128)} %reshape_reshape.3.s_ref), custom_call_target="tpu_custom_call" | custom-call | flops 3758096384 | bytes 17039360 | tf_op jit(solution)/shard_map/pallas_call | solution.py:54
  187.3 1.1 constant_dynamic-slice_fusion.1
  188.4 2.5 collective-permute-start.24
  191.6 1.3 collective-permute-start.22
  193.4 94.0 %collective-permute-done.24 = bf16[4,2,8,1024]{3,2,1,0:T(8,128)(2,1)S(1)} collective-permute-done((bf16[4,2,8,1024]{3,2,1,0:T(8,128)(2,1)S(1)}, bf16[4,2,8,1024]{3,2,1,0:T(8,128)(2,1)S(1)}, u32[]{:S(2)}, u32[]{:S(2)}) %collective-permute-start.24) | collective-permute-done | bytes 131104 | tf_op jit(solution)/shard_map/ppermute | solution.py:374
  287.4 1.5 collective-permute-done.22
  289.0 1.6 conditional.2
  289.0 1.6 broadcast.1832
  290.6 4.5 %shard_map.106 = bf16[16,112,1024]{2,1,0:T(8,128)(2,1)} custom-call(s32[16]{0:T(128)} %broadcast_clamp_fusion.index_ref, bf16[32,112,1024]{2,1,0:T(8,128)(2,1)} %bitcast.3.refs_0_, bf16[8,112,1024]{2,1,0:T(8,128)(2,1)} %collective-permute-done.20.refs_1_, bf16[8,112,1024]{2,1,0:T(8,128)(2,1)} %get-tuple-element.226.refs_2_), custom_call_target="tpu_custom_call" | custom-call | bytes 7340032 | tf_op jit(solution)/shard_map/pallas_call | solution.py:113
  295.1 4.8 %all-to-all-start.4 = ((bf16[16,112,1024]{2,1,0:T(8,128)(2,1)}), bf16[16,112,1024]{2,1,0:T(8,128)(2,1)}, u32[]{:S(2)}, u32[]{:S(2)}) async-start(bf16[16,112,1024]{2,1,0:T(8,128)(2,1)} %shard_map.106), calls=%async_computation.4 | async-start | bytes 7340032 | tf_op jit(solution)/shard_map/all_to_all | solution.py:389
  300.4 3.1 shard_map.107
  303.5 4.0 collective-permute-start.25
  307.6 1.8 collective-permute-start.26
  309.4 20.1 %collective-permute-done.26 = bf16[4,4,8,1024]{3,2,1,0:T(8,128)(2,1)S(1)} collective-permute-done((bf16[4,4,8,1024]{3,2,1,0:T(8,128)(2,1)S(1)}, bf16[4,4,8,1024]{3,2,1,0:T(8,128)(2,1)S(1)}, u32[]{:S(2)}, u32[]{:S(2)}) %collective-permute-start.26) | collective-permute-done | bytes 262176 | tf_op jit(solution)/shard_map/ppermute | solution.py:374
  329.6 1.7 collective-permute-start.28
  331.5 4.5 %collective-permute-done.28 = bf16[2,4,8,1024]{3,2,1,0:T(8,128)(2,1)S(1)} collective-permute-done((bf16[2,4,8,1024]{3,2,1,0:T(8,128)(2,1)S(1)}, bf16[2,4,8,1024]{3,2,1,0:T(8,128)(2,1)S(1)}, u32[]{:S(2)}, u32[]{:S(2)}) %collective-permute-start.28) | collective-permute-done | bytes 131104 | tf_op jit(solution)/shard_map/ppermute | solution.py:374
  336.0 1.9 collective-permute-done.29
  338.0 1.5 conditional.3
  338.0 1.5 broadcast.1847
  339.5 43.9 %collective-permute-done.25.refs_1_ = bf16[8,112,1024]{2,1,0:T(8,128)(2,1)S(1)} collective-permute-done((bf16[8,112,1024]{2,1,0:T(8,128)(2,1)}, bf16[8,112,1024]{2,1,0:T(8,128)(2,1)S(1)}, u32[]{:S(2)}, u32[]{:S(2)}) %collective-permute-start.25) | collective-permute-done | bytes 1835040 | tf_op jit(solution)/shard_map/ppermute | solution.py:385
  383.4 1.2 copy-done.1
  384.6 4.5 %shard_map.108 = bf16[16,112,1024]{2,1,0:T(8,128)(2,1)} custom-call(s32[16]{0:T(128)} %broadcast_clamp_fusion.index_ref, bf16[32,112,1024]{2,1,0:T(8,128)(2,1)} %bitcast.2.refs_0_, bf16[8,112,1024]{2,1,0:T(8,128)(2,1)} %copy-done.1, bf16[8,112,1024]{2,1,0:T(8,128)(2,1)} %get-tuple-element.227.refs_2_), custom_call_target="tpu_custom_call" | custom-call | bytes 7340032 | tf_op jit(solution)/shard_map/pallas_call | solution.py:113
  389.1 8.5 %all-to-all-start.3 = ((bf16[16,112,1024]{2,1,0:T(8,128)(2,1)}), bf16[16,112,1024]{2,1,0:T(8,128)(2,1)}, u32[]{:S(2)}, u32[]{:S(2)}) async-start(bf16[16,112,1024]{2,1,0:T(8,128)(2,1)} %shard_map.108), calls=%async_computation.3 | async-start | bytes 7340032 | tf_op jit(solution)/shard_map/all_to_all | solution.py:395
  400.5 1.0 fusion.1
  401.5 0.9 slice.85
  406.8 2.5 add_bitcast_fusion
  409.2 3.8 shard_map.109.refs_0_
  413.0 31.0 %all-to-all-done.3.blocks_ref = bf16[16,112,1024]{2,1,0:T(8,128)(2,1)} async-done(((bf16[16,112,1024]{2,1,0:T(8,128)(2,1)}), bf16[16,112,1024]{2,1,0:T(8,128)(2,1)}, u32[]{:S(2)}, u32[]{:S(2)}) %all-to-all-start.3) | async-done | bytes 3670048 | tf_op jit(solution)/shard_map/all_to_all | solution.py:395
  444.0 3.8 shard_map.110
  (119 shorter events, 18.4 us)
Async XLA Ops:
  4.1 10.1 %copy-start.2 = (bf16[16,3584]{1,0:T(8,128)(2,1)S(1)}, bf16[16,3584]{1,0:T(8,128)(2,1)}, u32[]{:S(2)}) copy-start(bf16[16,3584]{1,0:T(8,128)(2,1)} %param.28) | copy-start | bytes 344068
  4.1 10.1 %collective-permute-start.16 = (bf16[16,3712]{1,0:T(8,128)(2,1)S(1)}, bf16[16,3712]{1,0:T(8,128)(2,1)S(1)}, u32[]{:S(2)}, u32[]{:S(2)}) collective-permute-start(bf16[16,3712]{1,0:T(8,128)(2,1)S(1)} %pad_maximum_fusion.6), channel_id=1, source_target_pairs={{0,4},{1,5},{2,6},{3,7},{4,0},{5,1},{6,2},{7,3},{8,12},{9,13},{10,... | collective-permute-start | bytes 356360 | tf_op jit(solution)/shard_map/ppermute | solution.py:272
  14.2 7.3 %collective-permute-start.17 = (bf16[32,3712]{1,0:T(8,128)(2,1)S(1)}, bf16[32,3712]{1,0:T(8,128)(2,1)S(1)}, u32[]{:S(2)}, u32[]{:S(2)}) collective-permute-start(bf16[32,3712]{1,0:T(8,128)(2,1)S(1)} %pad_maximum_fusion.5), channel_id=1, source_target_pairs={{0,2},{1,3},{2,0},{3,1},{4,6},{5,7},{6,4},{7,5},{8,10},{9,11},{10,... | collective-permute-start | bytes 712712 | tf_op jit(solution)/shard_map/ppermute | solution.py:272
  22.2 13.1 %all-to-all-start = ((bf16[32,1,128]{2,1,0:T(2,128)(2,1)}), bf16[32,1,128]{2,1,0:T(2,128)(2,1)S(1)}, u32[]{:S(2)}, u32[]{:S(2)}) async-start(bf16[32,1,128]{2,1,0:T(2,128)(2,1)} %copy.142), calls=%async_computation | async-start | bytes 32768 | tf_op jit(solution)/shard_map/all_to_all | solution.py:283
  28.2 13.2 %collective-permute-start.18 = (bf16[64,3712]{1,0:T(8,128)(2,1)S(1)}, bf16[64,3712]{1,0:T(8,128)(2,1)S(1)}, u32[]{:S(2)}, u32[]{:S(2)}) collective-permute-start(bf16[64,3712]{1,0:T(8,128)(2,1)S(1)} %pad_maximum_fusion.4), channel_id=1, source_target_pairs={{0,1},{1,0},{2,3},{3,2},{4,5},{5,4},{6,7},{7,6},{8,9},{9,8},{10,11... | collective-permute-start | bytes 1425416 | tf_op jit(solution)/shard_map/ppermute | solution.py:272
  41.5 107.1 %all-to-all-start.2 = ((bf16[16,2,112,1024]{3,2,1,0:T(8,128)(2,1)}), bf16[16,2,112,1024]{3,2,1,0:T(8,128)(2,1)}, u32[]{:S(2)}, u32[]{:S(2)}) async-start(bf16[16,2,112,1024]{3,2,1,0:T(8,128)(2,1)} %shard_map.102), calls=%async_computation.2 | async-start | bytes 14680064 | tf_op jit(solution)/shard_map/all_to_all | solution.py:321
  52.3 96.1 %collective-permute-start.19 = (bf16[128,3712]{1,0:T(8,128)(2,1)S(1)}, bf16[128,3712]{1,0:T(8,128)(2,1)S(1)}, u32[]{:S(2)}, u32[]{:S(2)}) collective-permute-start(bf16[128,3712]{1,0:T(8,128)(2,1)S(1)} %pad_maximum_fusion.1), channel_id=1, source_target_pairs={{0,16},{1,17},{2,18},{3,19},{4,20},{5,21},{6,22},{7,23},{8,24},{9,... | collective-permute-start | bytes 2850824 | tf_op jit(solution)/shard_map/ppermute | solution.py:272
  148.6 146.5 %all-to-all-start.1 = ((bf16[16,2,112,1024]{3,2,1,0:T(8,128)(2,1)}), bf16[16,2,112,1024]{3,2,1,0:T(8,128)(2,1)}, u32[]{:S(2)}, u32[]{:S(2)}) async-start(bf16[16,2,112,1024]{3,2,1,0:T(8,128)(2,1)} %shard_map.103), calls=%async_computation.1 | async-start | bytes 14680064 | tf_op jit(solution)/shard_map/all_to_all | solution.py:321
  153.8 3.6 copy-start.4
  153.8 3.6 copy-start.3
  153.8 3.7 copy-start.5
  157.1 5.2 %collective-permute-start.21 = (bf16[256,3712]{1,0:T(8,128)(2,1)S(1)}, bf16[256,3712]{1,0:T(8,128)(2,1)}, u32[]{:S(2)}, u32[]{:S(2)}) collective-permute-start(bf16[256,3712]{1,0:T(8,128)(2,1)S(1)} %pad_maximum_fusion), channel_id=1, source_target_pairs={{0,8},{1,9},{2,10},{3,11},{4,12},{5,13},{6,14},{7,15},{8,0},{9,1},... | collective-permute-start | bytes 5701640 | tf_op jit(solution)/shard_map/ppermute | solution.py:272
  159.7 130.9 %collective-permute-start.20 = (bf16[8,112,1024]{2,1,0:T(8,128)(2,1)}, bf16[8,112,1024]{2,1,0:T(8,128)(2,1)}, u32[]{:S(2)}, u32[]{:S(2)}) collective-permute-start(bf16[8,112,1024]{2,1,0:T(8,128)(2,1)} %shard_map.104), channel_id=1, source_target_pairs={{0,4},{1,5},{2,6},{3,7},{4,0},{5,1},{6,2},{7,3},{8,12},{9,13},{10,... | collective-permute-start | bytes 5505032 | tf_op jit(solution)/shard_map/ppermute | solution.py:361
  164.1 1.8 copy-start
  188.4 99.0 %collective-permute-start.24 = (bf16[4,2,8,1024]{3,2,1,0:T(8,128)(2,1)S(1)}, bf16[4,2,8,1024]{3,2,1,0:T(8,128)(2,1)S(1)}, u32[]{:S(2)}, u32[]{:S(2)}) collective-permute-start(bf16[4,2,8,1024]{3,2,1,0:T(8,128)(2,1)S(1)} %get-tuple-element.215), channel_id=1, source_target_pairs={{0,6},{1,7},{2,4},{3,5},{4,2},{5,3},{6,0},{7,1},{8,14},{9,15},{10,... | collective-permute-start | bytes 393224 | tf_op jit(solution)/shard_map/ppermute | solution.py:374
  191.0 96.5 %collective-permute-start.23 = (bf16[4,2,8,1024]{3,2,1,0:T(8,128)(2,1)S(1)}, bf16[4,2,8,1024]{3,2,1,0:T(8,128)(2,1)S(1)}, u32[]{:S(2)}, u32[]{:S(2)}) collective-permute-start(bf16[4,2,8,1024]{3,2,1,0:T(8,128)(2,1)S(1)} %get-tuple-element.216), channel_id=1, source_target_pairs={{0,4},{1,5},{2,6},{3,7},{4,0},{5,1},{6,2},{7,3},{8,12},{9,13},{10,... | collective-permute-start | bytes 393224 | tf_op jit(solution)/shard_map/ppermute | solution.py:374
  191.6 97.3 %collective-permute-start.22 = (bf16[4,2,8,1024]{3,2,1,0:T(8,128)(2,1)S(1)}, bf16[4,2,8,1024]{3,2,1,0:T(8,128)(2,1)S(1)}, u32[]{:S(2)}, u32[]{:S(2)}) collective-permute-start(bf16[4,2,8,1024]{3,2,1,0:T(8,128)(2,1)S(1)} %get-tuple-element.217), channel_id=1, source_target_pairs={{0,2},{1,3},{2,0},{3,1},{4,6},{5,7},{6,4},{7,5},{8,10},{9,11},{10,... | collective-permute-start | bytes 393224 | tf_op jit(solution)/shard_map/ppermute | solution.py:374
  295.1 94.0 %all-to-all-start.4 = ((bf16[16,112,1024]{2,1,0:T(8,128)(2,1)}), bf16[16,112,1024]{2,1,0:T(8,128)(2,1)}, u32[]{:S(2)}, u32[]{:S(2)}) async-start(bf16[16,112,1024]{2,1,0:T(8,128)(2,1)} %shard_map.106), calls=%async_computation.4 | async-start | bytes 7340032 | tf_op jit(solution)/shard_map/all_to_all | solution.py:389
  303.5 79.9 %collective-permute-start.25 = (bf16[8,112,1024]{2,1,0:T(8,128)(2,1)}, bf16[8,112,1024]{2,1,0:T(8,128)(2,1)S(1)}, u32[]{:S(2)}, u32[]{:S(2)}) collective-permute-start(bf16[8,112,1024]{2,1,0:T(8,128)(2,1)} %shard_map.107), channel_id=1, source_target_pairs={{0,4},{1,5},{2,6},{3,7},{4,0},{5,1},{6,2},{7,3},{8,12},{9,13},{10,... | collective-permute-start | bytes 5505032 | tf_op jit(solution)/shard_map/ppermute | solution.py:385
  307.6 21.9 %collective-permute-start.26 = (bf16[4,4,8,1024]{3,2,1,0:T(8,128)(2,1)S(1)}, bf16[4,4,8,1024]{3,2,1,0:T(8,128)(2,1)S(1)}, u32[]{:S(2)}, u32[]{:S(2)}) collective-permute-start(bf16[4,4,8,1024]{3,2,1,0:T(8,128)(2,1)S(1)} %get-tuple-element.212), channel_id=1, source_target_pairs={{0,1},{1,0},{2,3},{3,2},{4,5},{5,4},{6,7},{7,6},{8,9},{9,8},{10,11... | collective-permute-start | bytes 786440 | tf_op jit(solution)/shard_map/ppermute | solution.py:374
  329.5 1.9 collective-permute-start.27
  329.6 6.4 %collective-permute-start.28 = (bf16[2,4,8,1024]{3,2,1,0:T(8,128)(2,1)S(1)}, bf16[2,4,8,1024]{3,2,1,0:T(8,128)(2,1)S(1)}, u32[]{:S(2)}, u32[]{:S(2)}) collective-permute-start(bf16[2,4,8,1024]{3,2,1,0:T(8,128)(2,1)S(1)} %get-tuple-element.210), channel_id=1, source_target_pairs={{0,16},{1,17},{2,18},{3,19},{4,20},{5,21},{6,22},{7,23},{8,24},{9,... | collective-permute-start | bytes 393224 | tf_op jit(solution)/shard_map/ppermute | solution.py:374
  331.3 6.6 %collective-permute-start.29 = (bf16[2,4,8,1024]{3,2,1,0:T(8,128)(2,1)S(1)}, bf16[2,4,8,1024]{3,2,1,0:T(8,128)(2,1)S(1)}, u32[]{:S(2)}, u32[]{:S(2)}) collective-permute-start(bf16[2,4,8,1024]{3,2,1,0:T(8,128)(2,1)S(1)} %get-tuple-element.211), channel_id=1, source_target_pairs={{0,24},{1,25},{2,26},{3,27},{4,28},{5,29},{6,30},{7,31},{8,16},{9,... | collective-permute-start | bytes 393224 | tf_op jit(solution)/shard_map/ppermute | solution.py:374
  383.4 1.2 copy-start.1
  389.1 10.4 %copy-start.6 = (s32[16,8]{0,1:T(8,128)S(1)}, s32[16,8]{0,1:T(8,128)}, u32[]{:S(2)}) copy-start(s32[16,8]{0,1:T(8,128)} %param.31) | copy-start | bytes 1540
  389.1 54.9 %all-to-all-start.3 = ((bf16[16,112,1024]{2,1,0:T(8,128)(2,1)}), bf16[16,112,1024]{2,1,0:T(8,128)(2,1)}, u32[]{:S(2)}, u32[]{:S(2)}) async-start(bf16[16,112,1024]{2,1,0:T(8,128)(2,1)} %shard_map.108), calls=%async_computation.3 | async-start | bytes 7340032 | tf_op jit(solution)/shard_map/all_to_all | solution.py:395
where the time goes:
time: 449 us; the launch traced here: 448 us
  waiting for transfers between devices  306 us (68%)
  starting transfers between devices  53.3 us (12%)
  Pallas kernels  47.7 us (11%)
  local copies, waits for them, and re-layouts  17.5 us (4%)
  other arithmetic  12.9 us (3%)
  matrix products  5.53 us (1%)
  between operations  4.61 us (1%)
    ppermute x7, waiting for transfers between devices, exchange(): got.append(lax.ppermute(block, AXES, pairs))  122 us
    ppermute x5, waiting for transfers between devices, double(): held = jnp.concatenate([held, lax.ppermute(held, AXES, pairs)], axis=0)  104 us
    ppermute x2, waiting for transfers between devices, per_device(): common = lax.ppermute(sent, AXES, over)  43.9 us
    all_to_all x1, waiting for transfers between devices, per_device(): lax.all_to_all(second, AXES, split_axis=0, concat_axis=0, tiled=True, axi...  31 us
    pallas_call x4, Pallas kernels, gather(): pl.pallas_call(gather_kernel, in_specs=[pl.BlockSpec(memory_space=pltpu.S...  15.3 us
    pallas_call x1, Pallas kernels, serve(): pl.pallas_call(expert_kernel, grid=(steps,), in_specs=[pl.BlockSpec((coun...  13 us
    pallas_call x2, Pallas kernels, by_chunk(): pl.pallas_call(functools.partial(chunk_kernel, first), in_specs=[anywhere...  11.9 us
    ppermute x5, starting transfers between devices, double(): held = jnp.concatenate([held, lax.ppermute(held, AXES, pairs)], axis=0)  9.84 us
  transfers between devices with their start and end apart: 19, of which 11 were waited for; matrix products, arithmetic and copies ran while one was open for 6% of the time, Pallas kernels for 10%

commit v1 on v0

--- a/solution.py
+++ b/solution.py
@@ -361,6 +361,7 @@
     common = lax.ppermute(sent, AXES, over)
     held = double(held, order[-1:])
     activated = work(held, place_all, primary_q, primary_scales)
+    leave_rows, activated = lax.optimization_barrier((leave_rows, activated))
 
     columns = dev_count // ROW_CHIPS
 
@@ -376,12 +377,12 @@
 
     blocks = activated.reshape(group_count, ROW_CHIPS, columns, holding * cells, hidden)
     blocks = exchange(blocks, 1, my_dev // columns, columns, 1)
-    leave_rows, blocks = lax.optimization_barrier((leave_rows, blocks))
     late = late_over(cross_count, leave_rows, first, over)
-    first = gather(give_rows, first, common, late)
-    first, leave_rows, blocks = lax.optimization_barrier((first, leave_rows, blocks))
+    leave_rows, late = lax.optimization_barrier((leave_rows, late))
     sent = gather(leave_rows[:COMMON], second)
     sent, blocks = lax.optimization_barrier((sent, blocks))
+    give_rows, _ = lax.optimization_barrier((give_rows, sent))
+    first = gather(give_rows, first, common, late)
     common = lax.ppermute(sent, AXES, over)
     blocks = exchange(blocks, 2, my_dev % columns, 1, 1)
     returned = exchange(blocks, 0, my_group, dev_count, 0)

time: 449 us -> 476 us (1.060); the launches traced: 448 us -> 482 us
  starting transfers between devices: 53.3 us -> 74.4 us
  waiting for transfers between devices: 306 us -> 314 us
  Pallas kernels: 47.7 us -> 52.8 us
    ppermute x0 -> x2, waiting for transfers between devices: none -> 142 us  [branch(): got = lax.ppermute(late, AXES, pairs)]
    ppermute x7, waiting for transfers between devices: 122 us -> 31.5 us  [exchange(): got.append(lax.ppermute(block, AXES, pairs))]
    ppermute x2, waiting for transfers between devices: 43.9 us -> 0.01 us  [per_device(): common = lax.ppermute(sent, AXES, over)]
    ppermute x0 -> x2, starting transfers between devices: none -> 25.9 us  [branch(): got = lax.ppermute(late, AXES, pairs)]
    pallas_call x4 -> x6, Pallas kernels: 15.3 us -> 20.3 us  [gather(): pl.pallas_call(gather_kernel, in_specs=[pl.BlockSpec(memory_space=pltpu.S...]
  transfers between devices with their start and end apart: 19 -> 21, of which waited for: 11 -> 10; matrix products, arithmetic and copies ran while one was open for 6% -> 6% of each run, Pallas kernels for 10% -> 9%
where the time goes in v1:
time: 476 us; the launch traced here: 482 us
  waiting for transfers between devices  314 us (66%)
  starting transfers between devices  74.4 us (16%)
  Pallas kernels  52.8 us (11%)
  local copies, waits for them, and re-layouts  16.3 us (3%)
  other arithmetic  14 us (3%)
  matrix products  5.58 us (1%)
    ppermute x2, waiting for transfers between devices, branch(): got = lax.ppermute(late, AXES, pairs)  142 us
    ppermute x5, waiting for transfers between devices, double(): held = jnp.concatenate([held, lax.ppermute(held, AXES, pairs)], axis=0)  104 us
    ppermute x7, waiting for transfers between devices, exchange(): got.append(lax.ppermute(block, AXES, pairs))  31.5 us
    all_to_all x1, waiting for transfers between devices, per_device(): lax.all_to_all(second, AXES, split_axis=0, concat_axis=0, tiled=True, axi...  31 us
    ppermute x2, starting transfers between devices, branch(): got = lax.ppermute(late, AXES, pairs)  25.9 us
    pallas_call x6, Pallas kernels, gather(): pl.pallas_call(gather_kernel, in_specs=[pl.BlockSpec(memory_space=pltpu.S...  20.3 us
    pallas_call x1, Pallas kernels, serve(): pl.pallas_call(expert_kernel, grid=(steps,), in_specs=[pl.BlockSpec((coun...  13 us
    pallas_call x2, Pallas kernels, by_chunk(): pl.pallas_call(functools.partial(chunk_kernel, first), in_specs=[anywhere...  11.9 us
  transfers between devices with their start and end apart: 21, of which 10 were waited for; matrix products, arithmetic and copies ran while one was open for 6% of the time, Pallas kernels for 9%

profile of v1, /device:TPU:0, one launch (start us, length us, event | category | flops | bytes accessed | tf_op | source)
XLA Modules:
  0.0 481.9 jit_solution(2171314891111982277)
XLA Ops:
  4.1 4.1 collective-permute-start.16
  8.2 6.0 %shard_map.102 = bf16[16,2,112,1024]{3,2,1,0:T(8,128)(2,1)} custom-call(bf16[2,3584,1024]{2,1,0:T(8,128)(2,1)} %q_ref.1), custom_call_target="tpu_custom_call" | custom-call | bytes 14680064 | tf_op jit(solution)/shard_map/pallas_call | solution.py:143
  14.2 1.6 collective-permute-start.17
  16.6 5.0 %collective-permute-done.17 = bf16[32,3712]{1,0:T(8,128)(2,1)S(1)} collective-permute-done((bf16[32,3712]{1,0:T(8,128)(2,1)S(1)}, bf16[32,3712]{1,0:T(8,128)(2,1)S(1)}, u32[]{:S(2)}, u32[]{:S(2)}) %collective-permute-start.17) | collective-permute-done | bytes 237600 | tf_op jit(solution)/shard_map/ppermute | solution.py:272
  22.2 6.0 %all-to-all-start = ((bf16[32,1,128]{2,1,0:T(2,128)(2,1)}), bf16[32,1,128]{2,1,0:T(2,128)(2,1)S(1)}, u32[]{:S(2)}, u32[]{:S(2)}) async-start(bf16[32,1,128]{2,1,0:T(2,128)(2,1)} %copy.142), calls=%async_computation | async-start | bytes 32768 | tf_op jit(solution)/shard_map/all_to_all | solution.py:283
  28.2 1.8 collective-permute-start.18
  30.1 5.2 %all-to-all-done = bf16[32,1,128]{2,1,0:T(2,128)(2,1)S(1)} async-done(((bf16[32,1,128]{2,1,0:T(2,128)(2,1)}), bf16[32,1,128]{2,1,0:T(2,128)(2,1)S(1)}, u32[]{:S(2)}, u32[]{:S(2)}) %all-to-all-start) | async-done | bytes 8224 | tf_op jit(solution)/shard_map/all_to_all | solution.py:283
  36.5 5.0 %collective-permute-done.18 = bf16[64,3712]{1,0:T(8,128)(2,1)S(1)} collective-permute-done((bf16[64,3712]{1,0:T(8,128)(2,1)S(1)}, bf16[64,3712]{1,0:T(8,128)(2,1)S(1)}, u32[]{:S(2)}, u32[]{:S(2)}) %collective-permute-start.18) | collective-permute-done | bytes 475168 | tf_op jit(solution)/shard_map/ppermute | solution.py:272
  41.5 4.8 %all-to-all-start.1 = ((bf16[16,2,112,1024]{3,2,1,0:T(8,128)(2,1)}), bf16[16,2,112,1024]{3,2,1,0:T(8,128)(2,1)}, u32[]{:S(2)}, u32[]{:S(2)}) async-start(bf16[16,2,112,1024]{3,2,1,0:T(8,128)(2,1)} %shard_map.102), calls=%async_computation.1 | async-start | bytes 14680064 | tf_op jit(solution)/shard_map/all_to_all | solution.py:321
  46.4 6.0 %shard_map.104 = bf16[16,2,112,1024]{3,2,1,0:T(8,128)(2,1)} custom-call(bf16[2,3584,1024]{2,1,0:T(8,128)(2,1)} %q_ref.1), custom_call_target="tpu_custom_call" | custom-call | bytes 14680064 | tf_op jit(solution)/shard_map/pallas_call | solution.py:143
  52.3 1.9 collective-permute-start.19
  54.3 94.2 %collective-permute-done.19 = bf16[128,3712]{1,0:T(8,128)(2,1)S(1)} collective-permute-done((bf16[128,3712]{1,0:T(8,128)(2,1)S(1)}, bf16[128,3712]{1,0:T(8,128)(2,1)S(1)}, u32[]{:S(2)}, u32[]{:S(2)}) %collective-permute-start.19) | collective-permute-done | bytes 950304 | tf_op jit(solution)/shard_map/ppermute | solution.py:272
  148.6 4.7 all-to-all-start.2
  153.8 3.2 shard_map.103
  159.7 2.5 collective-permute-start.29
  162.3 1.8 constant_dynamic-update-slice_fusion
  164.1 1.9 copy-done
  169.9 4.6 convolution_convert_fusion.x_ref
  174.5 13.0 %shard_map.105 = bf16[256,1024]{1,0:T(8,128)(2,1)} custom-call(bf16[256,3712]{1,0:T(8,128)(2,1)} %convolution_convert_fusion.x_ref, bf16[2,3584,1024]{2,1,0:T(8,128)(2,1)} %q_ref.1, f32[2,7,4,1024]{3,2,1,0:T(4,128)} %reshape_reshape.3.s_ref), custom_call_target="tpu_custom_call" | custom-call | flops 3758096384 | bytes 17039360 | tf_op jit(solution)/shard_map/pallas_call | solution.py:54
  187.5 1.1 constant_dynamic-slice_fusion.1
  188.6 2.5 collective-permute-start.23
  191.8 1.3 collective-permute-start.21
  193.1 107.3 %conditional.2 = (bf16[8,112,1024]{2,1,0:T(8,128)(2,1)}) conditional(s32[]{:T(128)} %clamp.21, () %tuple.81, (s32[16]{0:T(128)S(1)}, bf16[32,112,1024]{2,1,0:T(8,128)(2,1)}) %tuple.82, (s32[16]{0:T(128)S(1)}, bf16[32,112,1024]{2,1,0:T(8,128)(2,1)}) %tuple.82, (s32[16]{0:T(128)S(1)}, ...), branch_computations={%region_9.10_spmd, %region_10.11_spmd, %region_11.12_spmd, %region... | conditional | flops 8 | bytes 13074538 | solution.py:207
  193.6 2.4 branch_2_fun.2
  196.1 1.1 collective-permute-start.2
  197.2 101.7 %collective-permute-done.2 = bf16[2,112,1024]{2,1,0:T(8,128)(2,1)S(1)} collective-permute-done((bf16[2,112,1024]{2,1,0:T(8,128)(2,1)}, bf16[2,112,1024]{2,1,0:T(8,128)(2,1)S(1)}, u32[]{:S(2)}, u32[]{:S(2)}) %collective-permute-start.2) | collective-permute-done | bytes 458784 | tf_op jit(solution)/shard_map/cond/branch_2_fun/ppermute | solution.py:201
  298.9 1.5 pad.39
  300.9 3.2 shard_map.106
  304.7 4.5 shard_map.108
  309.2 6.6 %all-to-all-start.4 = ((bf16[16,112,1024]{2,1,0:T(8,128)(2,1)}), bf16[16,112,1024]{2,1,0:T(8,128)(2,1)}, u32[]{:S(2)}, u32[]{:S(2)}) async-start(bf16[16,112,1024]{2,1,0:T(8,128)(2,1)} %shard_map.108), calls=%async_computation.4 | async-start | bytes 7340032 | tf_op jit(solution)/shard_map/all_to_all | solution.py:390
  315.9 1.4 collective-permute-start.24
  317.3 1.8 collective-permute-start.25
  319.1 25.1 %collective-permute-done.25 = bf16[4,4,8,1024]{3,2,1,0:T(8,128)(2,1)S(1)} collective-permute-done((bf16[4,4,8,1024]{3,2,1,0:T(8,128)(2,1)S(1)}, bf16[4,4,8,1024]{3,2,1,0:T(8,128)(2,1)S(1)}, u32[]{:S(2)}, u32[]{:S(2)}) %collective-permute-start.25) | collective-permute-done | bytes 262176 | tf_op jit(solution)/shard_map/ppermute | solution.py:375
  344.4 1.5 collective-permute-start.27
  346.2 4.5 collective-permute-done.27
  350.7 1.9 collective-permute-done.28
  352.7 69.9 %conditional.3 = (bf16[8,112,1024]{2,1,0:T(8,128)(2,1)}) conditional(s32[]{:T(128)} %clamp.21, () %tuple.86, (s32[16]{0:T(128)S(1)}, bf16[32,112,1024]{2,1,0:T(8,128)(2,1)}) %tuple.88, (s32[16]{0:T(128)S(1)}, bf16[32,112,1024]{2,1,0:T(8,128)(2,1)}) %tuple.88, (s32[16]{0:T(128)S(1)}, ...), branch_computations={%region_18.19_spmd, %region_19.20_spmd, %region_20.21_spmd, %regio... | conditional | flops 8 | bytes 13074538 | solution.py:207
  353.3 2.4 branch_2_fun.3
  355.8 24.8 %collective-permute-start.9 = (bf16[2,112,1024]{2,1,0:T(8,128)(2,1)}, bf16[2,112,1024]{2,1,0:T(8,128)(2,1)S(1)}, u32[]{:S(2)}, u32[]{:S(2)}) collective-permute-start(bf16[2,112,1024]{2,1,0:T(8,128)(2,1)} %branch_2_fun.3), channel_id=1, source_target_pairs={{0,4},{1,5},{2,6},{3,7},{4,0},{5,1},{6,2},{7,3},{8,12},{9,13},{10,... | collective-permute-start | bytes 1376264 | tf_op jit(solution)/shard_map/cond/branch_2_fun/ppermute | solution.py:201
  380.6 40.6 %collective-permute-done.9 = bf16[2,112,1024]{2,1,0:T(8,128)(2,1)S(1)} collective-permute-done((bf16[2,112,1024]{2,1,0:T(8,128)(2,1)}, bf16[2,112,1024]{2,1,0:T(8,128)(2,1)S(1)}, u32[]{:S(2)}, u32[]{:S(2)}) %collective-permute-start.9) | collective-permute-done | bytes 458784 | tf_op jit(solution)/shard_map/cond/branch_2_fun/ppermute | solution.py:201
  421.1 1.5 pad.46
  422.6 4.5 shard_map.107
  427.2 4.5 all-to-all-start.3
  434.6 1.0 fusion.1
  440.8 2.4 add_bitcast_fusion
  443.2 3.8 shard_map.109.refs_0_
  447.0 31.0 %all-to-all-done.3.blocks_ref = bf16[16,112,1024]{2,1,0:T(8,128)(2,1)} async-done(((bf16[16,112,1024]{2,1,0:T(8,128)(2,1)}), bf16[16,112,1024]{2,1,0:T(8,128)(2,1)}, u32[]{:S(2)}, u32[]{:S(2)}) %all-to-all-start.3) | async-done | bytes 3670048 | tf_op jit(solution)/shard_map/all_to_all | solution.py:396
  478.0 3.8 shard_map.110
  (127 shorter events, 21.4 us)
Async XLA Ops:
  4.1 10.1 %copy-start.2 = (bf16[16,3584]{1,0:T(8,128)(2,1)S(1)}, bf16[16,3584]{1,0:T(8,128)(2,1)}, u32[]{:S(2)}) copy-start(bf16[16,3584]{1,0:T(8,128)(2,1)} %param.28) | copy-start | bytes 344068
  4.1 10.1 %collective-permute-start.16 = (bf16[16,3712]{1,0:T(8,128)(2,1)S(1)}, bf16[16,3712]{1,0:T(8,128)(2,1)S(1)}, u32[]{:S(2)}, u32[]{:S(2)}) collective-permute-start(bf16[16,3712]{1,0:T(8,128)(2,1)S(1)} %pad_maximum_fusion.6), channel_id=1, source_target_pairs={{0,4},{1,5},{2,6},{3,7},{4,0},{5,1},{6,2},{7,3},{8,12},{9,13},{10,... | collective-permute-start | bytes 356360 | tf_op jit(solution)/shard_map/ppermute | solution.py:272
  14.2 7.3 %collective-permute-start.17 = (bf16[32,3712]{1,0:T(8,128)(2,1)S(1)}, bf16[32,3712]{1,0:T(8,128)(2,1)S(1)}, u32[]{:S(2)}, u32[]{:S(2)}) collective-permute-start(bf16[32,3712]{1,0:T(8,128)(2,1)S(1)} %pad_maximum_fusion.5), channel_id=1, source_target_pairs={{0,2},{1,3},{2,0},{3,1},{4,6},{5,7},{6,4},{7,5},{8,10},{9,11},{10,... | collective-permute-start | bytes 712712 | tf_op jit(solution)/shard_map/ppermute | solution.py:272
  22.2 13.1 %all-to-all-start = ((bf16[32,1,128]{2,1,0:T(2,128)(2,1)}), bf16[32,1,128]{2,1,0:T(2,128)(2,1)S(1)}, u32[]{:S(2)}, u32[]{:S(2)}) async-start(bf16[32,1,128]{2,1,0:T(2,128)(2,1)} %copy.142), calls=%async_computation | async-start | bytes 32768 | tf_op jit(solution)/shard_map/all_to_all | solution.py:283
  28.2 13.2 %collective-permute-start.18 = (bf16[64,3712]{1,0:T(8,128)(2,1)S(1)}, bf16[64,3712]{1,0:T(8,128)(2,1)S(1)}, u32[]{:S(2)}, u32[]{:S(2)}) collective-permute-start(bf16[64,3712]{1,0:T(8,128)(2,1)S(1)} %pad_maximum_fusion.4), channel_id=1, source_target_pairs={{0,1},{1,0},{2,3},{3,2},{4,5},{5,4},{6,7},{7,6},{8,9},{9,8},{10,11... | collective-permute-start | bytes 1425416 | tf_op jit(solution)/shard_map/ppermute | solution.py:272
  41.5 107.1 %all-to-all-start.1 = ((bf16[16,2,112,1024]{3,2,1,0:T(8,128)(2,1)}), bf16[16,2,112,1024]{3,2,1,0:T(8,128)(2,1)}, u32[]{:S(2)}, u32[]{:S(2)}) async-start(bf16[16,2,112,1024]{3,2,1,0:T(8,128)(2,1)} %shard_map.102), calls=%async_computation.1 | async-start | bytes 14680064 | tf_op jit(solution)/shard_map/all_to_all | solution.py:321
  52.3 96.1 %collective-permute-start.19 = (bf16[128,3712]{1,0:T(8,128)(2,1)S(1)}, bf16[128,3712]{1,0:T(8,128)(2,1)S(1)}, u32[]{:S(2)}, u32[]{:S(2)}) collective-permute-start(bf16[128,3712]{1,0:T(8,128)(2,1)S(1)} %pad_maximum_fusion.1), channel_id=1, source_target_pairs={{0,16},{1,17},{2,18},{3,19},{4,20},{5,21},{6,22},{7,23},{8,24},{9,... | collective-permute-start | bytes 2850824 | tf_op jit(solution)/shard_map/ppermute | solution.py:272
  148.6 152.3 %all-to-all-start.2 = ((bf16[16,2,112,1024]{3,2,1,0:T(8,128)(2,1)}), bf16[16,2,112,1024]{3,2,1,0:T(8,128)(2,1)}, u32[]{:S(2)}, u32[]{:S(2)}) async-start(bf16[16,2,112,1024]{3,2,1,0:T(8,128)(2,1)} %shard_map.104), calls=%async_computation.2 | async-start | bytes 14680064 | tf_op jit(solution)/shard_map/all_to_all | solution.py:321
  153.8 3.6 copy-start.4
  153.8 3.7 copy-start.3
  153.8 3.8 copy-start.5
  157.1 5.2 %collective-permute-start.20 = (bf16[256,3712]{1,0:T(8,128)(2,1)S(1)}, bf16[256,3712]{1,0:T(8,128)(2,1)}, u32[]{:S(2)}, u32[]{:S(2)}) collective-permute-start(bf16[256,3712]{1,0:T(8,128)(2,1)S(1)} %pad_maximum_fusion), channel_id=1, source_target_pairs={{0,8},{1,9},{2,10},{3,11},{4,12},{5,13},{6,14},{7,15},{8,0},{9,1},... | collective-permute-start | bytes 5701640 | tf_op jit(solution)/shard_map/ppermute | solution.py:272
  159.7 145.0 %collective-permute-start.29 = (bf16[8,112,1024]{2,1,0:T(8,128)(2,1)}, bf16[8,112,1024]{2,1,0:T(8,128)(2,1)}, u32[]{:S(2)}, u32[]{:S(2)}) collective-permute-start(bf16[8,112,1024]{2,1,0:T(8,128)(2,1)} %shard_map.103), channel_id=1, source_target_pairs={{0,4},{1,5},{2,6},{3,7},{4,0},{5,1},{6,2},{7,3},{8,12},{9,13},{10,... | collective-permute-start | bytes 5505032 | tf_op jit(solution)/shard_map/ppermute | solution.py:361
  164.1 2.0 copy-start
  188.6 115.5 %collective-permute-start.23 = (bf16[4,2,8,1024]{3,2,1,0:T(8,128)(2,1)S(1)}, bf16[4,2,8,1024]{3,2,1,0:T(8,128)(2,1)S(1)}, u32[]{:S(2)}, u32[]{:S(2)}) collective-permute-start(bf16[4,2,8,1024]{3,2,1,0:T(8,128)(2,1)S(1)} %get-tuple-element.215), channel_id=1, source_target_pairs={{0,6},{1,7},{2,4},{3,5},{4,2},{5,3},{6,0},{7,1},{8,14},{9,15},{10,... | collective-permute-start | bytes 393224 | tf_op jit(solution)/shard_map/ppermute | solution.py:375
  191.1 113.0 %collective-permute-start.22 = (bf16[4,2,8,1024]{3,2,1,0:T(8,128)(2,1)S(1)}, bf16[4,2,8,1024]{3,2,1,0:T(8,128)(2,1)S(1)}, u32[]{:S(2)}, u32[]{:S(2)}) collective-permute-start(bf16[4,2,8,1024]{3,2,1,0:T(8,128)(2,1)S(1)} %get-tuple-element.216), channel_id=1, source_target_pairs={{0,4},{1,5},{2,6},{3,7},{4,0},{5,1},{6,2},{7,3},{8,12},{9,13},{10,... | collective-permute-start | bytes 393224 | tf_op jit(solution)/shard_map/ppermute | solution.py:375
  191.8 112.3 %collective-permute-start.21 = (bf16[4,2,8,1024]{3,2,1,0:T(8,128)(2,1)S(1)}, bf16[4,2,8,1024]{3,2,1,0:T(8,128)(2,1)S(1)}, u32[]{:S(2)}, u32[]{:S(2)}) collective-permute-start(bf16[4,2,8,1024]{3,2,1,0:T(8,128)(2,1)S(1)} %get-tuple-element.217), channel_id=1, source_target_pairs={{0,2},{1,3},{2,0},{3,1},{4,6},{5,7},{6,4},{7,5},{8,10},{9,11},{10,... | collective-permute-start | bytes 393224 | tf_op jit(solution)/shard_map/ppermute | solution.py:375
  196.1 102.8 %collective-permute-start.2 = (bf16[2,112,1024]{2,1,0:T(8,128)(2,1)}, bf16[2,112,1024]{2,1,0:T(8,128)(2,1)S(1)}, u32[]{:S(2)}, u32[]{:S(2)}) collective-permute-start(bf16[2,112,1024]{2,1,0:T(8,128)(2,1)} %branch_2_fun.2), channel_id=1, source_target_pairs={{0,4},{1,5},{2,6},{3,7},{4,0},{5,1},{6,2},{7,3},{8,12},{9,13},{10,... | collective-permute-start | bytes 1376264 | tf_op jit(solution)/shard_map/cond/branch_2_fun/ppermute | solution.py:201
  309.2 6.7 %copy-start.1 = (bf16[8,112,1024]{2,1,0:T(8,128)(2,1)S(1)}, bf16[8,112,1024]{2,1,0:T(8,128)(2,1)}, u32[]{:S(2)}) copy-start(bf16[8,112,1024]{2,1,0:T(8,128)(2,1)} %shard_map.106) | copy-start | bytes 5505028
  309.2 117.9 %all-to-all-start.4 = ((bf16[16,112,1024]{2,1,0:T(8,128)(2,1)}), bf16[16,112,1024]{2,1,0:T(8,128)(2,1)}, u32[]{:S(2)}, u32[]{:S(2)}) async-start(bf16[16,112,1024]{2,1,0:T(8,128)(2,1)} %shard_map.108), calls=%async_computation.4 | async-start | bytes 7340032 | tf_op jit(solution)/shard_map/all_to_all | solution.py:390
  315.9 106.7 %collective-permute-start.24 = (bf16[8,112,1024]{2,1,0:T(8,128)(2,1)S(1)}, bf16[8,112,1024]{2,1,0:T(8,128)(2,1)}, u32[]{:S(2)}, u32[]{:S(2)}) collective-permute-start(bf16[8,112,1024]{2,1,0:T(8,128)(2,1)S(1)} %copy-done.1), channel_id=1, source_target_pairs={{0,4},{1,5},{2,6},{3,7},{4,0},{5,1},{6,2},{7,3},{8,12},{9,13},{10,... | collective-permute-start | bytes 5505032 | tf_op jit(solution)/shard_map/ppermute | solution.py:386
  317.3 27.0 %collective-permute-start.25 = (bf16[4,4,8,1024]{3,2,1,0:T(8,128)(2,1)S(1)}, bf16[4,4,8,1024]{3,2,1,0:T(8,128)(2,1)S(1)}, u32[]{:S(2)}, u32[]{:S(2)}) collective-permute-start(bf16[4,4,8,1024]{3,2,1,0:T(8,128)(2,1)S(1)} %get-tuple-element.212), channel_id=1, source_target_pairs={{0,1},{1,0},{2,3},{3,2},{4,5},{5,4},{6,7},{7,6},{8,9},{9,8},{10,11... | collective-permute-start | bytes 786440 | tf_op jit(solution)/shard_map/ppermute | solution.py:375
  344.3 1.9 collective-permute-start.26
  344.4 6.4 %collective-permute-start.27 = (bf16[2,4,8,1024]{3,2,1,0:T(8,128)(2,1)S(1)}, bf16[2,4,8,1024]{3,2,1,0:T(8,128)(2,1)S(1)}, u32[]{:S(2)}, u32[]{:S(2)}) collective-permute-start(bf16[2,4,8,1024]{3,2,1,0:T(8,128)(2,1)S(1)} %get-tuple-element.210), channel_id=1, source_target_pairs={{0,16},{1,17},{2,18},{3,19},{4,20},{5,21},{6,22},{7,23},{8,24},{9,... | collective-permute-start | bytes 393224 | tf_op jit(solution)/shard_map/ppermute | solution.py:375
  345.9 6.7 %collective-permute-start.28 = (bf16[2,4,8,1024]{3,2,1,0:T(8,128)(2,1)S(1)}, bf16[2,4,8,1024]{3,2,1,0:T(8,128)(2,1)S(1)}, u32[]{:S(2)}, u32[]{:S(2)}) collective-permute-start(bf16[2,4,8,1024]{3,2,1,0:T(8,128)(2,1)S(1)} %get-tuple-element.211), channel_id=1, source_target_pairs={{0,24},{1,25},{2,26},{3,27},{4,28},{5,29},{6,30},{7,31},{8,16},{9,... | collective-permute-start | bytes 393224 | tf_op jit(solution)/shard_map/ppermute | solution.py:375
  355.8 65.4 %collective-permute-start.9 = (bf16[2,112,1024]{2,1,0:T(8,128)(2,1)}, bf16[2,112,1024]{2,1,0:T(8,128)(2,1)S(1)}, u32[]{:S(2)}, u32[]{:S(2)}) collective-permute-start(bf16[2,112,1024]{2,1,0:T(8,128)(2,1)} %branch_2_fun.3), channel_id=1, source_target_pairs={{0,4},{1,5},{2,6},{3,7},{4,0},{5,1},{6,2},{7,3},{8,12},{9,13},{10,... | collective-permute-start | bytes 1376264 | tf_op jit(solution)/shard_map/cond/branch_2_fun/ppermute | solution.py:201
  427.1 6.5 %copy-start.6 = (s32[16,8]{0,1:T(8,128)S(1)}, s32[16,8]{0,1:T(8,128)}, u32[]{:S(2)}) copy-start(s32[16,8]{0,1:T(8,128)} %param.31) | copy-start | bytes 1540
  427.2 50.8 %all-to-all-start.3 = ((bf16[16,112,1024]{2,1,0:T(8,128)(2,1)}), bf16[16,112,1024]{2,1,0:T(8,128)(2,1)}, u32[]{:S(2)}, u32[]{:S(2)}) async-start(bf16[16,112,1024]{2,1,0:T(8,128)(2,1)} %shard_map.107), calls=%async_computation.3 | async-start | bytes 7340032 | tf_op jit(solution)/shard_map/all_to_all | solution.py:396
